TPU v7x, 32 devices: a whole 2x2x4 slice. The times are simulated.
32 devices in a mesh: groups: 2 (over y), ep: 4 (over z), tp: 4 (over x, core).
Axes of the slice: x: 2, y: 2, z: 4, core: 2. Of those that a mesh axis runs over, the one named last changes fastest.
Arguments:
- queries: bfloat16 [192, 6144], P(('groups', 'ep'), 'tp'), parts along dimension 0, may hold values from -16 to 16
- cached_key_rows: bfloat16 [192, 128, 1024], P(('groups', 'ep'), None, 'tp'), parts along dimension 0, may hold values from -16 to 16
- cached_value_rows: bfloat16 [192, 128, 1024], P(('groups', 'ep'), None, 'tp'), parts along dimension 0, may hold values from -6 to 6
- lengths: int32 [192], P(('groups', 'ep')), parts along dimension 0, may hold values from 2 to 128, as said below
- out_weight: bfloat16 [6144, 6144], P('ep', 'tp'), may hold values from -0.078125 to 0.078125
- residual: bfloat16 [192, 6144], P(('groups', 'ep'), 'tp'), parts along dimension 0, may hold values from -6 to 6
- norm_gain: float32 [6144], P('tp'), may hold values from 0.5 to 2
- routes: int32 [192, 4], P(('groups', 'ep')), parts along dimension 0, may hold values from 0 to 15, all different within a row; in each aligned block of 24 rows (0 to 23, 24 to 47, ...) at most 14 rows name the same one
- route_gates: float32 [192, 4], P(('groups', 'ep')), parts along dimension 0, may hold values from 0.5 to 1.5
- gate_up_weight: bfloat16 [2, 6144, 2, 10752], P(None, 'tp', None, 'ep'), may hold values from -0.078125 to 0.078125
- down_weight: bfloat16 [2, 10752, 6144], P(None, 'ep', 'tp'), may hold values from -0.0625 to 0.0625
Outputs:
- mixed: bfloat16 [192, 6144], P(('groups', 'ep'), 'tp'), parts along dimension 0
There are 2 independent parts, one for each index of `groups`. A program takes and returns all parts, laid end to end along the dimension named above; an argument that names none is the same for every part. Nothing has to cross between parts.
Inputs may be any that keep to these rules, and one draw needn't show every extreme that they name: `lengths`: some row has exactly 128 live positions. `routes`: each row names 4 different ids; in each aligned block of 24 rows no id is named by more than 14 rows, a bound that some block reaches.
All inputs are finite; a program needn't handle non-finite values.
Results may differ from a plain program's by a relative error of at most 0.015.
Values may be sent and summed in bfloat16 or wider, within the bound.
A program may use at most 192 MiB of HBM per device.

v0:
```python
import jax
import jax.numpy as jnp
from jax import lax
from jax.sharding import PartitionSpec as P

D = 6144
HEAD_WIDTH = 128
EXP_WIN = 2
CAP = 14


def local(
    queries,
    cached_key_rows,
    cached_value_rows,
    lengths,
    out_weight,
    residual,
    norm_gain,
    routes,
    route_gates,
    gate_up_weight,
    down_weight,
):
    row_count = queries.shape[0]
    head_count = queries.shape[1] // HEAD_WIDTH
    kv_count = cached_key_rows.shape[2] // HEAD_WIDTH
    query_group_width = head_count // kv_count
    cache_len = cached_key_rows.shape[1]
    per_head_queries = queries.reshape(row_count, kv_count, query_group_width, HEAD_WIDTH)
    per_head_keys = cached_key_rows.reshape(row_count, cache_len, kv_count, HEAD_WIDTH)
    per_head_values = cached_value_rows.reshape(row_count, cache_len, kv_count, HEAD_WIDTH)
    scores = jnp.einsum(
        "tkgd,tskd->tkgs", per_head_queries, per_head_keys, preferred_element_type=jnp.float32
    ) * HEAD_WIDTH ** (-0.5)
    live = jnp.arange(cache_len, dtype=jnp.int32)[None, :] < lengths[:, None]
    scores = jnp.where(live[:, None, None, :], scores, -1e30)
    row_max = jnp.max(scores, axis=-1, keepdims=True)
    expon = jnp.exp(scores - row_max)
    probs = (expon / jnp.sum(expon, axis=-1, keepdims=True)).astype(jnp.bfloat16)
    weighted = jnp.einsum(
        "tkgs,tskd->tkgd", probs, per_head_values, preferred_element_type=jnp.float32
    )
    attended = weighted.astype(jnp.bfloat16).reshape(row_count, head_count * HEAD_WIDTH)
    full_rows = lax.all_gather(attended, "tp", axis=1, tiled=True)
    feature_slices = lax.all_to_all(full_rows, "ep", split_axis=1, concat_axis=0, tiled=True)
    projected = lax.psum_scatter(
        jnp.dot(feature_slices, out_weight, preferred_element_type=jnp.float32).astype(
            jnp.bfloat16
        ),
        "ep",
        scatter_dimension=0,
        tiled=True,
    ).astype(jnp.float32)
    stream = residual.astype(jnp.float32) + projected
    square_total = lax.psum(jnp.sum(stream * stream, axis=-1), "tp")
    normed = (stream * lax.rsqrt(square_total[:, None] / D + 1e-05) * norm_gain[None, :]).astype(
        jnp.bfloat16
    )
    expert_ids = jnp.arange(EXP_WIN, dtype=jnp.int32)
    matches = routes[:, :, None] == expert_ids[None, None, :]
    chosen = jnp.any(matches, axis=1)
    chosen_int = chosen.astype(jnp.int32)
    slot_index = jnp.cumsum(chosen_int, axis=0) - chosen_int
    slot_ids = jnp.arange(CAP, dtype=jnp.int32)[:, None, None]
    placement_map = (chosen[None, :, :] & (slot_index[None, :, :] == slot_ids)).astype(jnp.float32)
    buffers = jnp.einsum(
        "cte,td->ced",
        placement_map.astype(jnp.bfloat16),
        normed,
        preferred_element_type=jnp.float32,
    ).astype(jnp.bfloat16)
    partial_pre = jnp.einsum(
        "ced,edgf->cegf",
        lax.all_gather(buffers, "ep", axis=0, tiled=True),
        gate_up_weight,
        preferred_element_type=jnp.float32,
    )
    summed = lax.psum(partial_pre.astype(jnp.bfloat16), "tp").astype(jnp.float32)
    hidden = (jax.nn.silu(summed[:, :, 0]) * summed[:, :, 1]).astype(jnp.bfloat16)
    expert_out = lax.psum_scatter(
        jnp.einsum("cef,efd->ced", hidden, down_weight, preferred_element_type=jnp.float32).astype(
            jnp.bfloat16
        ),
        "ep",
        scatter_dimension=0,
        tiled=True,
    ).astype(jnp.float32)
    gate_weights = jnp.sum(route_gates[:, :, None] * matches.astype(jnp.float32), axis=1)
    combined = jnp.einsum(
        "cte,ced->td",
        placement_map * gate_weights[None, :, :],
        expert_out,
        precision=lax.Precision.HIGHEST,
    )
    return (stream + combined).astype(jnp.bfloat16)


def solution(mesh):
    in_specs = (
        P(("groups", "ep"), "tp"),
        P(("groups", "ep"), None, "tp"),
        P(("groups", "ep"), None, "tp"),
        P(("groups", "ep")),
        P("ep", "tp"),
        P(("groups", "ep"), "tp"),
        P("tp"),
        P(("groups", "ep"), None),
        P(("groups", "ep"), None),
        P(None, "tp", None, "ep"),
        P(None, "ep", "tp"),
    )
    out_specs = P(("groups", "ep"), "tp")
    return jax.shard_map(local, mesh=mesh, in_specs=in_specs, out_specs=out_specs, check_vma=False)
```

profile of v0, /device:TPU:0, one launch (start us, length us, event | category | flops | bytes accessed | tf_op | source)
XLA Modules:
  0.0 190.7 jit_solution(5403763561017129131)
XLA Ops:
  6.5 0.0 copy-start
  6.5 0.0 copy-start.6
  6.5 0.0 reduce-scatter.2.cloned.1.call-start
  6.5 1.1 reshape.55
  7.7 0.7 iota_compare_fusion.1
  8.4 0.0 copy-done
  8.4 0.9 fusion.24
  9.3 0.2 fusion.52
  9.6 0.0 copy-done.6
  9.6 0.7 fusion.28
  10.3 0.1 reshape.58
  10.4 7.4 %all_gather.6 = bf16[24,6144]{1,0:T(8,128)(2,1)S(1)} all-gather(bf16[24,1536]{1,0:T(8,128)(2,1)S(1)} %reshape.58), channel_id=1, replica_groups=mesh['groups'=2,'ep'=4,'tp'=4] {'tp'}, dimensions={1}, use_global_device_ids=true | all-gather | bytes 368640 | tf_op jit(solution)/shard_map/all_gather | solution.py:45
  17.8 14.8 %all_to_all.19 = bf16[24,4,1536]{2,0,1:T(8,128)(2,1)S(1)} all-to-all(bf16[24,4,1536]{2,0,1:T(8,128)(2,1)S(1)} %bitcast.64), channel_id=1, replica_groups=mesh['groups'=2,'ep'=4,'tp'=4] {'ep'}, dimensions={1} | all-to-all | bytes 589824 | tf_op jit(solution)/shard_map/all_to_all | solution.py:46
  32.5 0.0 copy-start.4
  32.5 0.0 copy-start.1
  32.6 0.0 copy-start.3
  32.6 4.0 %convolution_convert_fusion.1 = bf16[96,1536]{1,0:T(8,128)(2,1)} fusion(bf16[96,1536]{1,0:T(8,128)(2,1)S(1)} %bitcast.65, bf16[1536,1536]{1,0:T(8,128)(2,1)} %param.15), kind=kOutput, calls=%fused_computation.6 | convolution fusion | flops 453132288 | bytes 5308416 | tf_op jit(solution)/shard_map/dot_general | solution.py:48
  36.5 0.0 reduce-scatter.2.cloned.1.call-update
  36.6 0.0 all-reduce.4.cloned.1.call-start
  36.6 0.0 copy-done.4
  36.6 0.1 copy.45
  36.8 0.1 copy.47
  36.9 18.8 %reduce-scatter.2.cloned.1.call-done = bf16[24,1536]{1,0:T(8,128)(2,1)} async-done(((bf16[96,1536]{1,0:T(8,128)(2,1)}), bf16[24,1536]{1,0:T(8,128)(2,1)}) %reduce-scatter.2.cloned.1.call-update) | async-done | bytes 73744 | tf_op jit(solution)/shard_map/reduce_scatter | solution.py:47
  55.6 0.0 copy-done.1
  55.6 1.0 multiply_reduce_fusion
  56.7 5.7 %psum.14 = f32[24]{0:T(128)S(1)} all-reduce(f32[24]{0:T(128)S(1)} %multiply_reduce_fusion), channel_id=1, replica_groups=mesh['groups'=2,'ep'=4,'tp'=4] {'tp'}, use_global_device_ids=true, to_apply=%region_7.8 | all-reduce | flops 24 | bytes 192 | tf_op jit(solution)/shard_map/psum | solution.py:56
  62.3 0.0 copy-done.3
  62.3 1.1 convolution_convert_fusion.2
  63.5 0.1 copy.48
  63.6 14.8 %all_gather.7 = bf16[56,2,1536]{2,1,0:T(2,128)(2,1)S(1)} all-gather(bf16[14,2,1536]{2,1,0:T(2,128)(2,1)S(1)} %copy.48), channel_id=1, replica_groups=mesh['groups'=2,'ep'=4,'tp'=4] {'ep'}, dimensions={0}, use_global_device_ids=true | all-gather | bytes 430080 | tf_op jit(solution)/shard_map/all_gather | solution.py:75
  78.3 19.8 %fusion.6 = bf16[56,2,2,2688]{3,0,2,1:T(8,128)(2,1)} fusion(bf16[2,1536,2,2688]{3,2,1,0:T(2,128)(2,1)} %param.20, bf16[56,2,1536,1]{2,1,0,3:T(2,128)(2,1)S(1)} %bitcast.62), kind=kOutput, calls=%fused_computation.4 | convolution fusion | flops 1850290176 | bytes 34578432 | tf_op jit(solution)/shard_map/ced,edgf->cegf/dot_general | solution.py:73
  98.1 0.0 all-reduce.4.cloned.1.call-update
  98.2 0.0 all-reduce.6.cloned.1.call-start
  98.2 36.3 %all-reduce.4.cloned.1.call-done = bf16[56,2,2,2688]{3,0,2,1:T(8,128)(2,1)} async-done(((bf16[56,2,2,2688]{3,0,2,1:T(8,128)(2,1)}), bf16[56,2,2,2688]{3,0,2,1:T(8,128)(2,1)}) %all-reduce.4.cloned.1.call-update) | async-done | bytes 1204240 | tf_op jit(solution)/shard_map/psum | solution.py:79
  134.5 1.4 convert_element_type.73
  136.0 0.0 copy-start.7
  136.0 0.0 copy-start.5
  136.0 0.0 copy-start.2
  136.0 8.6 %fusion.9 = bf16[56,2,1536]{2,0,1:T(8,128)(2,1)S(1)} fusion(bf16[2,2688,1536]{2,1,0:T(8,128)(2,1)} %param.21, f32[56,2,2,2688]{3,0,2,1:T(8,128)S(1)} %convert_element_type.73), kind=kOutput, calls=%fused_computation.7 | convolution fusion | flops 926822400 | bytes 19267584 | tf_op jit(solution)/shard_map/cef,efd->ced/dot_general | solution.py:82
  144.6 1.0 copy.52
  145.6 0.0 all-reduce.6.cloned.1.call-update
  145.7 0.0 copy-done.7
  145.7 0.6 dynamic-slice
  146.9 0.0 copy-done.5
  146.9 35.4 %all-reduce.6.cloned.1.call-done = bf16[56,2,1536]{2,1,0:T(2,128)(2,1)} async-done(((bf16[56,2,1536]{2,1,0:T(2,128)(2,1)}), bf16[56,2,1536]{2,1,0:T(2,128)(2,1)}) %all-reduce.6.cloned.1.call-update) | async-done | bytes 344080
  182.3 0.9 constant_dynamic-slice_fusion
  183.3 0.0 copy-done.2
  183.3 0.9 fusion.11
  (7 shorter events, 0.1 us)
Async XLA Ops:
  6.5 1.9 copy-start
  6.5 3.0 %copy-start.6 = (bf16[24,128,256]{2,1,0:T(8,128)(2,1)S(1)}, bf16[24,128,256]{2,1,0:T(8,128)(2,1)}, u32[]{:S(2)}) copy-start(bf16[24,128,256]{2,1,0:T(8,128)(2,1)} %param.13) | copy-start | bytes 4718596
  6.5 49.1 %reduce-scatter.2.cloned.1.call-start = ((), (), s32[]{:S(2)}) async-start(), calls=%async_computation.2 | async-start | bytes 368640 | tf_op jit(solution)/shard_map/reduce_scatter | solution.py:47
  32.5 4.1 %copy-start.4 = (s32[24,4]{0,1:T(4,128)S(1)}, s32[24,4]{0,1:T(4,128)}, u32[]{:S(2)}) copy-start(s32[24,4]{0,1:T(4,128)} %param.18) | copy-start | bytes 1156
  32.5 23.1 %copy-start.1 = (bf16[24,1536]{1,0:T(8,128)(2,1)S(1)}, bf16[24,1536]{1,0:T(8,128)(2,1)}, u32[]{:S(2)}) copy-start(bf16[24,1536]{1,0:T(8,128)(2,1)} %param.16) | copy-start | bytes 221188
  32.6 29.8 %copy-start.3 = (f32[1536]{0:T(1024)S(1)}, f32[1536]{0:T(1024)}, u32[]{:S(2)}) copy-start(f32[1536]{0:T(1024)} %param.17) | copy-start | bytes 18436
  36.6 98.0 %all-reduce.4.cloned.1.call-start = ((), (), s32[]{:S(2)}) async-start(), calls=%async_computation.3 | async-start | bytes 2408448 | tf_op jit(solution)/shard_map/psum | solution.py:79
  98.2 84.1 %all-reduce.6.cloned.1.call-start = ((), (), s32[]{:S(2)}) async-start(), calls=%async_computation.4 | async-start | bytes 688128
  136.0 9.7 %copy-start.7 = (u32[32]{0:T(128)S(1)}, u32[32]{0:T(128)}, u32[]{:S(2)}) copy-start(u32[32]{0:T(128)} %constant.26) | copy-start | bytes 388
  136.0 10.9 %copy-start.5 = (f32[24,4]{0,1:T(4,128)S(1)}, f32[24,4]{0,1:T(4,128)}, u32[]{:S(2)}) copy-start(f32[24,4]{0,1:T(4,128)} %param.19) | copy-start | bytes 1156
  136.0 47.3 %copy-start.2 = (bf16[24,1536]{1,0:T(8,128)(2,1)S(1)}, bf16[24,1536]{1,0:T(8,128)(2,1)}, u32[]{:S(2)}) copy-start(bf16[24,1536]{1,0:T(8,128)(2,1)} %reduce-scatter.2.cloned.1.call-done) | copy-start | bytes 221188
Sparse Core Ops, SparseCore 0:
  36.7 18.9 reduce-scatter.1
  98.3 36.1 all-reduce.3
  145.8 36.4 all-reduce.5
where the time goes:
time: 191 us
  waiting for transfers between devices  90.5 us (47%)
  blocking collectives  42.5 us (22%)
  matrix products  36 us (19%)
  between operations  13.9 us (7%)
  local copies, waits for them, and re-layouts  4.09 us (2%)
  other arithmetic  3.54 us (2%)
    psum x1, waiting for transfers between devices, local(): lax.psum(partial_pre.astype(jnp.bfloat16), 'tp').astype(jnp.float32)  36.3 us
    unnamed x4, waiting for transfers between devices  35.4 us
    dot_general x1, matrix products, local(): jnp.einsum('ced,edgf->cegf', lax.all_gather(buffers, 'ep', axis=0, tiled=...  19.8 us
    reduce_scatter x1, waiting for transfers between devices, local(): lax.psum_scatter(jnp.dot(feature_slices, out_weight, preferred_element_ty...  18.8 us
    all_to_all x1, blocking collectives, local(): lax.all_to_all(full_rows, 'ep', split_axis=1, concat_axis=0, tiled=True)  14.8 us
    all_gather x1, blocking collectives, local(): lax.all_gather(buffers, 'ep', axis=0, tiled=True)  14.8 us
    dot_general x1, matrix products, local(): jnp.einsum('cef,efd->ced', hidden, down_weight, preferred_element_type=jn...  8.61 us
    all_gather x1, blocking collectives, local(): full_rows = lax.all_gather(attended, 'tp', axis=1, tiled=True)  7.37 us
  transfers between devices with their start and end apart: 3, of which 3 were waited for; matrix products, arithmetic and copies ran while one was open for 0% of the time, Pallas kernels for 0%

commit v1 on v0

--- a/solution.py
+++ b/solution.py
@@ -1,6 +1,8 @@
 import jax
 import jax.numpy as jnp
 from jax import lax
+from jax.experimental import pallas as pl
+from jax.experimental.pallas import tpu as pltpu
 from jax.sharding import PartitionSpec as P
 
 D = 6144
@@ -96,6 +98,465 @@
     return (stream + combined).astype(jnp.bfloat16)
 
 
+MESH = pl.DeviceIdType.MESH
+ROWS = 24
+PAIR = 2 * ROWS
+HALF = 768
+N = 4
+SLOTS = N * CAP
+LANE = 128
+TILES = 21
+SIDE = 11
+STEP = 10
+WIDE = SIDE * LANE
+K = 2 * HALF
+
+
+def bf(x):
+    return x.astype(jnp.bfloat16)
+
+
+def f32(x):
+    return x.astype(jnp.float32)
+
+
+def mm(a, b):
+    return jnp.dot(a, b, preferred_element_type=jnp.float32)
+
+
+def fused(
+    att_ref,
+    meta_ref,
+    res_ref,
+    gain_ref,
+    wo_hbm,
+    gu_hbm,
+    wd_hbm,
+    out_ref,
+    wo,
+    gu,
+    wd,
+    a_send,
+    a_recv,
+    part,
+    rs_send,
+    rs_recv,
+    meta_all,
+    y_all,
+    ss_all,
+    stream,
+    xp,
+    s_mine,
+    s_recv,
+    l1_send,
+    l1_recv,
+    acc,
+    l2_send,
+    l2_recv,
+    hid,
+    outs,
+    c_send,
+    c_recv,
+    wo_sem,
+    gu_sem,
+    wd_sem,
+    a_ss,
+    a_rs,
+    m_ss,
+    m_rs,
+    rs_ss,
+    rs_rs,
+    y_ss,
+    y_rs,
+    q_ss,
+    q_rs,
+    s_ss,
+    s_rs,
+    l1_ss,
+    l1_rs,
+    l2_ss,
+    l2_rs,
+    h_ss,
+    h_rs,
+    c_ss,
+    c_rs,
+):
+    g, i, j = lax.axis_index("groups"), lax.axis_index("ep"), lax.axis_index("tp")
+    x, c = j // 2, j % 2
+    sibling = (g, i, x * 2 + (1 - c))
+    across = (g, i, (1 - x) * 2 + c)
+
+    def remote(src, dst, ss, rs, dev):
+        return pltpu.make_async_remote_copy(
+            src_ref=src, dst_ref=dst, send_sem=ss, recv_sem=rs, device_id=dev, device_id_type=MESH
+        )
+
+    barrier = pltpu.get_barrier_semaphore()
+    me = i * N + j
+    for d in range(1, N * N):
+        other = (me + d) % (N * N)
+        pl.semaphore_signal(
+            barrier, inc=1, device_id=(g, other // N, other % N), device_id_type=MESH
+        )
+
+    wo_copy = pltpu.make_async_copy(wo_hbm, wo, wo_sem)
+    wo_copy.start()
+
+    def gu_copy(e, t):
+        return pltpu.make_async_copy(
+            gu_hbm.at[e, :, :, pl.ds(pl.multiple_of(t * LANE, LANE), LANE)],
+            gu.at[e * TILES + t],
+            gu_sem.at[e * TILES + t],
+        )
+
+    def wd_copy(e):
+        return pltpu.make_async_copy(wd_hbm.at[e], wd.at[e], wd_sem.at[e])
+
+    a_send[0:ROWS, :] = att_ref[:, 0:HALF]
+    a_send[ROWS:PAIR, :] = att_ref[:, HALF:K]
+    meta_all[i] = meta_ref[...]
+
+    pl.semaphore_wait(barrier, N * N - 1)
+
+    for d in (1, 2, 3):
+        remote(a_send, a_recv.at[i], a_ss.at[d], a_rs.at[i], (g, j, (j + d) % N)).start()
+
+    @pl.when(i != j)
+    def _():
+        remote(a_send, a_recv.at[i], a_ss.at[0], a_rs.at[i], (g, j, j)).start()
+
+    @pl.when(i == j)
+    def _():
+        a_recv[i] = a_send[...]
+
+    for d in (1, 2, 3):
+        remote(
+            meta_all.at[i], meta_all.at[i], m_ss.at[d], m_rs.at[i], (g, (i + d) % N, j)
+        ).start()
+
+    for e in (1 - c, c):
+
+        @pl.loop(0, TILES)
+        def _(t, e=e):
+            gu_copy(e, t).start()
+
+    for e in range(EXP_WIN):
+        wd_copy(e).start()
+
+    for d in range(N):
+        s = (i + d) % N
+
+        @pl.when(jnp.logical_or(d != 0, i != j))
+        def _(s=s):
+            remote(a_send, a_recv.at[s], a_ss.at[0], a_rs.at[s], sibling).wait_recv()
+
+    wo_copy.wait()
+    lhs = [
+        jnp.concatenate([a_recv[k, ROWS * h : ROWS * (h + 1), :] for k in range(N)], axis=0)
+        for h in range(2)
+    ]
+    for n in range(2):
+        cols = slice(HALF * n, HALF * (n + 1))
+        r = mm(lhs[0], wo[0:HALF, cols]) + mm(lhs[1], wo[HALF:K, cols])
+        part[:, cols] = r
+        for k in range(N):
+            rs_send[k, ROWS * n : ROWS * (n + 1), :] = bf(r[ROWS * k : ROWS * (k + 1), :])
+    for d in (2, 1, 3):
+        k = (i + d) % N
+        remote(rs_send.at[k], rs_recv.at[i], rs_ss.at[d], rs_rs.at[i], (g, k, j)).start()
+    mine = pl.ds(pl.multiple_of(i * ROWS, 8), ROWS)
+    stream[...] = f32(res_ref[...]) + part[mine, :]
+    for d in (1, 3, 2):
+        s = (i + d) % N
+        remote(rs_send.at[s], rs_recv.at[s], rs_ss.at[d], rs_rs.at[s], sibling).wait_recv()
+        got = f32(rs_recv[s])
+        stream[:, 0:HALF] += got[0:ROWS]
+        stream[:, HALF:K] += got[ROWS:PAIR]
+
+    st = stream[...]
+    y = bf(st * gain_ref[...])
+    y_all[i] = jnp.concatenate([y[:, 0:HALF], y[:, HALF:K]], axis=0)
+    ss_all[i] = jnp.broadcast_to(jnp.sum(st * st, axis=1, keepdims=True), (ROWS, LANE))
+    for d in (2, 1, 3):
+        dev = (g, (i + d) % N, j)
+        remote(y_all.at[i], y_all.at[i], y_ss.at[d], y_rs.at[i], dev).start()
+        remote(ss_all.at[i], ss_all.at[i], q_ss.at[d], q_rs.at[i], dev).start()
+    for d in (1, 3, 2):
+        s = (i + d) % N
+        remote(meta_all.at[s], meta_all.at[s], m_ss.at[d], m_rs.at[s], sibling).wait_recv()
+        remote(ss_all.at[s], ss_all.at[s], q_ss.at[d], q_rs.at[s], sibling).wait_recv()
+        remote(y_all.at[s], y_all.at[s], y_ss.at[d], y_rs.at[s], sibling).wait_recv()
+
+    ydat = [
+        jnp.concatenate([y_all[k, ROWS * h : ROWS * (h + 1), :] for k in range(N)], axis=0)
+        for h in range(2)
+    ]
+    ssd = jnp.concatenate([ss_all[k] for k in range(N)], axis=0)
+    twice = bf(
+        lax.broadcasted_iota(jnp.int32, (LANE, 2 * LANE), 1) // 2
+        == lax.broadcasted_iota(jnp.int32, (LANE, 2 * LANE), 0)
+    )
+    keep = (
+        lax.broadcasted_iota(jnp.int32, (2 * SLOTS, 2 * LANE), 1) % 2
+        == lax.broadcasted_iota(jnp.int32, (2 * SLOTS, 2 * LANE), 0) // SLOTS
+    )
+
+    def spots(e):
+        return jnp.concatenate(
+            [meta_all[k, ROWS * e : ROWS * (e + 1), :] for k in range(N)], axis=0
+        )
+
+    for e in range(EXP_WIN):
+        place = spots(e)
+        place_t = jnp.transpose(
+            jnp.concatenate([place, jnp.zeros((LANE - N * ROWS, LANE), jnp.float32)], axis=0)
+        )[0 : 2 * SLOTS, 0 : N * ROWS]
+        s_mine[e] = jnp.dot(
+            place_t, ssd, precision=lax.Precision.HIGHEST, preferred_element_type=jnp.float32
+        )
+        place_b = bf(place_t)
+        for h in range(2):
+            rows = bf(mm(place_b, ydat[h]))
+            for q in range(HALF // LANE):
+                both = mm(rows[:, LANE * q : LANE * (q + 1)], twice)
+                at = 2 * (HALF * h + LANE * q)
+                xp[e, :, at : at + 2 * LANE] = bf(jnp.where(keep, both, 0.0))
+
+    s_one = remote(s_mine.at[1 - c], s_recv.at[0], s_ss.at[0], s_rs.at[0], sibling)
+    s_one.start()
+
+    def product(e, h, p, width):
+        t = e * TILES + h * STEP + 2 * p
+        w = [gu.at[t + k].reshape(2 * K, LANE)[...] for k in range(width)]
+        w = w[0] if width == 1 else jnp.concatenate(w, axis=1)
+        return mm(xp[e], w)
+
+    def sweep(e, h, store):
+        @pl.loop(0, SIDE // 2)
+        def _(p):
+            at = pl.ds(pl.multiple_of(p * 2 * LANE, 2 * LANE), 2 * LANE)
+            store(at, product(e, h, p, 2))
+
+        store(pl.ds((SIDE - 1) * LANE, LANE), product(e, h, SIDE // 2, 1))
+
+    def arrive(e):
+        @pl.loop(0, TILES)
+        def _(t):
+            gu_copy(e, t).wait()
+
+    arrive(1 - c)
+    for n, h in enumerate((1 - x, x)):
+
+        def to_sibling(at, r, n=n):
+            l1_send[n, :, at] = bf(r)
+
+        sweep(1 - c, h, to_sibling)
+        remote(l1_send.at[n], l1_recv.at[n], l1_ss.at[n], l1_rs.at[n], sibling).start()
+    arrive(c)
+    s_one.wait_recv()
+    s_mine[c] = s_mine[c] + s_recv[0]
+    s_two = remote(s_mine.at[c], s_recv.at[1], s_ss.at[1], s_rs.at[1], across)
+    s_two.start()
+    first = remote(l1_send.at[0], l1_recv.at[0], l1_ss.at[0], l1_rs.at[0], sibling)
+    first.wait_recv()
+
+    def to_across(at, r):
+        l2_send[:, at] = bf(r + f32(l1_recv[0, :, at]))
+
+    sweep(c, 1 - x, to_across)
+    l2 = remote(l2_send, l2_recv, l2_ss, l2_rs, across)
+    l2.start()
+    second = remote(l1_send.at[1], l1_recv.at[1], l1_ss.at[1], l1_rs.at[1], sibling)
+    second.wait_recv()
+
+    def to_own(at, r):
+        acc[:, at] = r + f32(l1_recv[1, :, at])
+
+    sweep(c, x, to_own)
+    s_two.wait_recv()
+    scale = lax.rsqrt((s_mine[c] + s_recv[1])[0:SLOTS, 0:1] / D + 1e-05)
+    l2.wait_recv()
+
+    @pl.loop(0, SIDE)
+    def _(t):
+        at = pl.ds(pl.multiple_of(t * LANE, LANE), LANE)
+        total = acc[:, at] + f32(l2_recv[:, at])
+        gate, up = total[0:SLOTS] * scale, total[SLOTS : 2 * SLOTS] * scale
+        value = gate / (1.0 + jnp.exp(-gate)) * up
+        value = jnp.where(jnp.logical_and(t == 0, x == 1), 0.0, value)
+        hid[c, x, :, at] = bf(
+            jnp.concatenate([value, jnp.zeros((64 - SLOTS, LANE), jnp.float32)], axis=0)
+        )
+
+    h_sib = remote(hid.at[c, x], hid.at[c, x], h_ss.at[0], h_rs.at[0], sibling)
+    h_acr = remote(hid.at[c, x], hid.at[c, x], h_ss.at[1], h_rs.at[1], across)
+    h_acr.start()
+    h_sib.start()
+    for e in range(EXP_WIN):
+        wd_copy(e).wait()
+
+    def down(e, h, n):
+        rows = pl.ds(pl.multiple_of(h * STEP * LANE, LANE), WIDE)
+        return mm(hid[e, h], wd[e, rows, 512 * n : 512 * (n + 1)])
+
+    for n in range(3):
+        outs[c, :, 512 * n : 512 * (n + 1)] = down(c, x, n)
+    h_sib.wait_recv()
+    for n in range(3):
+        outs[1 - c, :, 512 * n : 512 * (n + 1)] = down(1 - c, x, n)
+    h_acr.wait_recv()
+    h_fwd = remote(hid.at[c, 1 - x], hid.at[c, 1 - x], h_ss.at[2], h_rs.at[2], sibling)
+    h_fwd.start()
+    for n in range(3):
+        outs[c, :, 512 * n : 512 * (n + 1)] += down(c, 1 - x, n)
+    h_fwd.wait_recv()
+    for n in range(3):
+        outs[1 - c, :, 512 * n : 512 * (n + 1)] += down(1 - c, 1 - x, n)
+
+    gates = jnp.concatenate([meta_all[k, 2 * ROWS : 3 * ROWS, :] for k in range(N)], axis=0)
+    live = lax.broadcasted_iota(jnp.int32, (N * ROWS, 64), 1) < SLOTS
+    picks = [bf(jnp.where(live, spots(e)[:, 0:64], 0.0)) for e in range(EXP_WIN)]
+    for n in range(2):
+        cols = slice(HALF * n, HALF * (n + 1))
+        r = gates[:, 0:1] * mm(picks[0], bf(outs[0, :, cols]))
+        r = r + gates[:, 1:2] * mm(picks[1], bf(outs[1, :, cols]))
+        part[:, cols] = r
+        for k in range(N):
+            c_send[k, ROWS * n : ROWS * (n + 1), :] = bf(r[ROWS * k : ROWS * (k + 1), :])
+    for d in (2, 1, 3):
+        k = (i + d) % N
+        remote(c_send.at[k], c_recv.at[i], c_ss.at[d], c_rs.at[i], (g, k, j)).start()
+    stream[...] += part[mine, :]
+    for d in (1, 3, 2):
+        s = (i + d) % N
+        remote(c_send.at[s], c_recv.at[s], c_ss.at[d], c_rs.at[s], sibling).wait_recv()
+        got = f32(c_recv[s])
+        stream[:, 0:HALF] += got[0:ROWS]
+        stream[:, HALF:K] += got[ROWS:PAIR]
+    out_ref[...] = bf(stream[...])
+
+    for d in (1, 2, 3):
+        remote(a_send, a_recv.at[i], a_ss.at[d], a_rs.at[i], sibling).wait_send()
+        remote(meta_all.at[i], meta_all.at[i], m_ss.at[d], m_rs.at[i], sibling).wait_send()
+        k = (i + d) % N
+        remote(rs_send.at[k], rs_recv.at[i], rs_ss.at[d], rs_rs.at[i], sibling).wait_send()
+        remote(y_all.at[i], y_all.at[i], y_ss.at[d], y_rs.at[i], sibling).wait_send()
+        remote(ss_all.at[i], ss_all.at[i], q_ss.at[d], q_rs.at[i], sibling).wait_send()
+        remote(c_send.at[k], c_recv.at[i], c_ss.at[d], c_rs.at[i], sibling).wait_send()
+
+    @pl.when(i != j)
+    def _():
+        remote(a_send, a_recv.at[i], a_ss.at[0], a_rs.at[i], sibling).wait_send()
+
+    for copy in (s_one, s_two, first, second, l2, h_sib, h_acr, h_fwd):
+        copy.wait_send()
+
+
+def attention(queries, cached_key_rows, cached_value_rows, lengths):
+    row_count = queries.shape[0]
+    head_count = queries.shape[1] // HEAD_WIDTH
+    kv_count = cached_key_rows.shape[2] // HEAD_WIDTH
+    query_group_width = head_count // kv_count
+    cache_len = cached_key_rows.shape[1]
+    per_head_queries = queries.reshape(row_count, kv_count, query_group_width, HEAD_WIDTH)
+    per_head_keys = cached_key_rows.reshape(row_count, cache_len, kv_count, HEAD_WIDTH)
+    per_head_values = cached_value_rows.reshape(row_count, cache_len, kv_count, HEAD_WIDTH)
+    scores = jnp.einsum(
+        "tkgd,tskd->tkgs", per_head_queries, per_head_keys, preferred_element_type=jnp.float32
+    ) * HEAD_WIDTH ** (-0.5)
+    live = jnp.arange(cache_len, dtype=jnp.int32)[None, :] < lengths[:, None]
+    scores = jnp.where(live[:, None, None, :], scores, -1e30)
+    row_max = jnp.max(scores, axis=-1, keepdims=True)
+    expon = jnp.exp(scores - row_max)
+    probs = (expon / jnp.sum(expon, axis=-1, keepdims=True)).astype(jnp.bfloat16)
+    weighted = jnp.einsum(
+        "tkgs,tskd->tkgd", probs, per_head_values, preferred_element_type=jnp.float32
+    )
+    return weighted.astype(jnp.bfloat16).reshape(row_count, head_count * HEAD_WIDTH)
+
+
+def placement(routes, route_gates):
+    matches = routes[:, :, None] == jnp.arange(EXP_WIN, dtype=jnp.int32)[None, None, :]
+    chosen = jnp.any(matches, axis=1)
+    earlier = jnp.arange(ROWS)[:, None] > jnp.arange(ROWS)[None, :]
+    slot = jnp.sum(earlier[:, :, None] & chosen[None, :, :], axis=1, dtype=jnp.int32)
+    position = jnp.where(chosen, lax.axis_index("ep") * CAP + slot, -1)
+    lanes = jnp.arange(LANE, dtype=jnp.int32)
+    lanes = jnp.where(lanes < 2 * SLOTS, lanes % SLOTS, -2)
+    spots = (position.T[:, :, None] == lanes[None, None, :]).astype(jnp.float32)
+    gates = jnp.sum(route_gates[:, :, None] * matches.astype(jnp.float32), axis=1)
+    gates = jnp.pad(gates, ((0, 0), (0, LANE - EXP_WIN)))
+    return jnp.concatenate([spots.reshape(EXP_WIN * ROWS, LANE), gates], axis=0)
+
+
+def fused_local(
+    queries,
+    cached_key_rows,
+    cached_value_rows,
+    lengths,
+    out_weight,
+    residual,
+    norm_gain,
+    routes,
+    route_gates,
+    gate_up_weight,
+    down_weight,
+):
+    attended = attention(queries, cached_key_rows, cached_value_rows, lengths)
+    meta = placement(routes, route_gates)
+    b16, f4 = jnp.bfloat16, jnp.float32
+    vmem, hbm = pl.BlockSpec(memory_space=pltpu.VMEM), pl.BlockSpec(memory_space=pl.ANY)
+    dma = pltpu.SemaphoreType.DMA
+    scratch = [
+        pltpu.VMEM((K, K), b16),
+        pltpu.VMEM((EXP_WIN * TILES, K, 2, LANE), b16),
+        pltpu.VMEM((EXP_WIN, TILES * LANE, K), b16),
+        pltpu.VMEM((PAIR, HALF), b16),
+        pltpu.VMEM((N, PAIR, HALF), b16),
+        pltpu.VMEM((N * ROWS, K), f4),
+        pltpu.VMEM((N, PAIR, HALF), b16),
+        pltpu.VMEM((N, PAIR, HALF), b16),
+        pltpu.VMEM((N, 3 * ROWS, LANE), f4),
+        pltpu.VMEM((N, PAIR, HALF), b16),
+        pltpu.VMEM((N, ROWS, LANE), f4),
+        pltpu.VMEM((ROWS, K), f4),
+        pltpu.VMEM((EXP_WIN, 2 * SLOTS, 2 * K), b16),
+        pltpu.VMEM((EXP_WIN, 2 * SLOTS, LANE), f4),
+        pltpu.VMEM((2, 2 * SLOTS, LANE), f4),
+        pltpu.VMEM((2, 2 * SLOTS, WIDE), b16),
+        pltpu.VMEM((2, 2 * SLOTS, WIDE), b16),
+        pltpu.VMEM((2 * SLOTS, WIDE), f4),
+        pltpu.VMEM((2 * SLOTS, WIDE), b16),
+        pltpu.VMEM((2 * SLOTS, WIDE), b16),
+        pltpu.VMEM((EXP_WIN, 2, 64, WIDE), b16),
+        pltpu.VMEM((EXP_WIN, 64, K), f4),
+        pltpu.VMEM((N, PAIR, HALF), b16),
+        pltpu.VMEM((N, PAIR, HALF), b16),
+        dma,
+        dma((EXP_WIN * TILES,)),
+        dma((EXP_WIN,)),
+    ]
+    scratch += [dma((N,))] * 10 + [dma((2,))] * 4 + [dma, dma] + [dma((3,))] * 2 + [dma((N,))] * 2
+    return pl.pallas_call(
+        fused,
+        out_shape=jax.ShapeDtypeStruct((ROWS, K), b16),
+        in_specs=[vmem] * 4 + [hbm] * 3,
+        out_specs=vmem,
+        scratch_shapes=scratch,
+        compiler_params=pltpu.CompilerParams(
+            collective_id=0, has_side_effects=True, vmem_limit_bytes=VMEM_BYTES
+        ),
+    )(attended, meta, residual, norm_gain[None, :], out_weight, gate_up_weight, down_weight)
+
+
+VMEM_BYTES = 63 << 20
+
+
+def pick(mesh):
+    fits = mesh.shape["ep"] == N and mesh.shape["tp"] == N
+    return fused_local if fits else local
+
+
 def solution(mesh):
     in_specs = (
         P(("groups", "ep"), "tp"),
@@ -111,4 +572,4 @@
         P(None, "ep", "tp"),
     )
     out_specs = P(("groups", "ep"), "tp")
-    return jax.shard_map(local, mesh=mesh, in_specs=in_specs, out_specs=out_specs, check_vma=False)
+    return jax.shard_map(pick(mesh), mesh=mesh, in_specs=in_specs, out_specs=out_specs, check_vma=False)

time: 191 us -> 90.3 us (0.47)
  waiting for transfers between devices: 90.5 us -> 0 us
  Pallas kernels: 0 us -> 81 us
  blocking collectives: 42.5 us -> 0 us
  matrix products: 36 us -> 3 us
  between operations: 13.9 us -> 0.05 us
    pallas_call x0 -> x1, Pallas kernels: none -> 81 us  [fused_local(): pl.pallas_call(fused, out_shape=jax.ShapeDtypeStruct((ROWS, K), b16), in_...]
    psum x1 -> x0, waiting for transfers between devices: 36.3 us -> none  [local(): lax.psum(partial_pre.astype(jnp.bfloat16), 'tp').astype(jnp.float32)]
    unnamed x4 -> x0, waiting for transfers between devices: 35.4 us -> none
    dot_general x7 -> x2, matrix products: 36 us -> 3 us  [the longest x1 2.31 us: attention(): jnp.einsum('tkgd,tskd->tkgs', per_head_queries, per_head_keys, preferred_...]
    all_gather x2 -> x0, blocking collectives: 22.1 us -> none  [the longest x1 14.8 us: local(): lax.all_gather(buffers, 'ep', axis=0, tiled=True)]
    reduce_scatter x1 -> x0, waiting for transfers between devices: 18.8 us -> none  [local(): lax.psum_scatter(jnp.dot(feature_slices, out_weight, preferred_element_ty...]
    all_to_all x1 -> x0, blocking collectives: 14.8 us -> none  [local(): lax.all_to_all(full_rows, 'ep', split_axis=1, concat_axis=0, tiled=True)]
    psum x1 -> x0, blocking collectives: 5.66 us -> none  [local(): square_total = lax.psum(jnp.sum(stream * stream, axis=-1), 'tp')]
  transfers between devices with their start and end apart: 3 -> 0, of which waited for: 3 -> 0; matrix products, arithmetic and copies ran while one was open for 0% -> 0% of each run, Pallas kernels for 0% -> 0%
where the time goes in v1:
time: 90.3 us; the launch traced here: 90.1 us
  Pallas kernels  81 us (90%)
  local copies, waits for them, and re-layouts  4.15 us (5%)
  matrix products  3 us (3%)
  other arithmetic  1.85 us (2%)
    pallas_call x1, Pallas kernels, fused_local(): pl.pallas_call(fused, out_shape=jax.ShapeDtypeStruct((ROWS, K), b16), in_...  81 us
    dot_general x1, matrix products, attention(): jnp.einsum('tkgd,tskd->tkgs', per_head_queries, per_head_keys, preferred_...  2.31 us

profile of v1, /device:TPU:0, one launch (start us, length us, event | category | flops | bytes accessed | tf_op | source)
XLA Modules:
  0.0 90.1 jit_solution(17735487593797807432)
XLA Ops:
  0.0 0.0 copy-start.3
  0.0 1.1 %reshape.62 = bf16[24,2,6,128]{3,2,1,0:T(8,128)(2,1)S(1)} reshape(bf16[24,1536]{1,0:T(8,128)(2,1)} %param.11) | data formatting | bytes 147456 | tf_op jit(solution)/shard_map/reshape | solution.py:461
  1.1 0.7 iota_compare_fusion.2
  1.8 2.3 %fusion.11 = f32[24,2,6,128]{3,2,1,0:T(8,128)S(1)} fusion(bf16[24,2,6,128]{3,2,1,0:T(8,128)(2,1)S(1)} %reshape.62, pred[24,128]{1,0:T(8,128)(4,1)S(1)} %iota_compare_fusion.2, bf16[24,128,256]{2,1,0:T(8,128)(2,1)} %param.12), kind=kOutput, calls=%fused_computation.9 | convolution fusion | flops 9510912 | bytes 1797120 | tf_op jit(solution)/shard_map/tkgd,tskd->tkgs/dot_general | solution.py:464
  4.2 0.0 copy-start.1
  4.2 0.0 copy-start.2
  4.2 0.0 copy-start
  4.2 0.3 fusion.20
  4.4 0.0 copy-done.3
  4.4 0.7 fusion.15
  5.1 0.7 reshape.65.att_ref
  5.9 0.0 copy-done.1
  5.9 0.1 convert_reduce_fusion
  6.0 0.1 eq.34
  6.1 0.1 compare_convert_fusion
  6.2 0.0 copy-done.2
  6.2 0.1 copy.24
  6.3 0.6 select_maximum_fusion.meta_ref
  6.9 0.0 copy-done
  6.9 0.6 broadcast_in_dim.26.gain_ref
  7.5 81.0 %shard_map.109 = bf16[24,1536]{1,0:T(8,128)(2,1)} custom-call(bf16[24,1536]{1,0:T(8,128)(2,1)} %reshape.65.att_ref, f32[72,128]{1,0:T(8,128)} %select_maximum_fusion.meta_ref, bf16[24,1536]{1,0:T(8,128)(2,1)} %res_ref.1, f32[1,1536]{1,0:T(1,128)} %broadcast_in_dim.26.gain_ref, bf16[1536,1536]{1,0:T(8,128)(2,1)} %wo_hbm.1, bf16[2,1536,2,2688]{3,2,1,0:T(2,128)(2,1)} %gu_hbm.1, ...), custom_call_target="tpu_custom_call" | custom-call | tf_op jit(solution)/shard_map/pallas_call | solution.py:540
  88.6 1.5 %copy.42 = bf16[24,1536]{1,0:T(8,128)(2,1)} copy(bf16[24,1536]{1,0:T(8,128)(2,1)} %shard_map.109) | data formatting | bytes 147456
  (5 shorter events, 0.1 us)
Async XLA Ops:
  0.0 4.4 %copy-start.3 = (bf16[24,128,256]{2,1,0:T(8,128)(2,1)S(1)}, bf16[24,128,256]{2,1,0:T(8,128)(2,1)}, u32[]{:S(2)}) copy-start(bf16[24,128,256]{2,1,0:T(8,128)(2,1)} %param.13) | copy-start | bytes 4718596
  4.2 1.7 %copy-start.1 = (s32[24,4]{0,1:T(4,128)S(1)}, s32[24,4]{0,1:T(4,128)}, u32[]{:S(2)}) copy-start(s32[24,4]{0,1:T(4,128)} %param.18) | copy-start | bytes 1156
  4.2 2.0 %copy-start.2 = (f32[24,4]{0,1:T(4,128)S(1)}, f32[24,4]{0,1:T(4,128)}, u32[]{:S(2)}) copy-start(f32[24,4]{0,1:T(4,128)} %param.19) | copy-start | bytes 1156
  4.2 2.8 %copy-start = (f32[1536]{0:T(1024)S(1)}, f32[1536]{0:T(1024)}, u32[]{:S(2)}) copy-start(f32[1536]{0:T(1024)} %param.17) | copy-start | bytes 18436

commit v2 on v1

--- a/solution.py
+++ b/solution.py
@@ -176,8 +176,12 @@
     l1_rs,
     l2_ss,
     l2_rs,
+    hs_ss,
+    hs_rs,
     h_ss,
     h_rs,
+    f_ss,
+    f_rs,
     c_ss,
     c_rs,
 ):
@@ -201,16 +205,29 @@
 
     wo_copy = pltpu.make_async_copy(wo_hbm, wo, wo_sem)
     wo_copy.start()
+    gu_flat = gu_hbm.reshape(EXP_WIN * 2 * K, TILES * LANE)
 
     def gu_copy(e, t):
         return pltpu.make_async_copy(
-            gu_hbm.at[e, :, :, pl.ds(pl.multiple_of(t * LANE, LANE), LANE)],
+            gu_flat.at[
+                pl.ds(pl.multiple_of(e * 2 * K, 2 * K), 2 * K),
+                pl.ds(pl.multiple_of(t * LANE, LANE), LANE),
+            ],
             gu.at[e * TILES + t],
             gu_sem.at[e * TILES + t],
         )
 
     def wd_copy(e):
         return pltpu.make_async_copy(wd_hbm.at[e], wd.at[e], wd_sem.at[e])
+
+    for e in (1 - c, c):
+
+        @pl.loop(0, TILES)
+        def _(t, e=e):
+            gu_copy(e, t).start()
+
+    for e in range(EXP_WIN):
+        wd_copy(e).start()
 
     a_send[0:ROWS, :] = att_ref[:, 0:HALF]
     a_send[ROWS:PAIR, :] = att_ref[:, HALF:K]
@@ -233,15 +250,6 @@
         remote(
             meta_all.at[i], meta_all.at[i], m_ss.at[d], m_rs.at[i], (g, (i + d) % N, j)
         ).start()
-
-    for e in (1 - c, c):
-
-        @pl.loop(0, TILES)
-        def _(t, e=e):
-            gu_copy(e, t).start()
-
-    for e in range(EXP_WIN):
-        wd_copy(e).start()
 
     for d in range(N):
         s = (i + d) % N
@@ -327,7 +335,7 @@
 
     def product(e, h, p, width):
         t = e * TILES + h * STEP + 2 * p
-        w = [gu.at[t + k].reshape(2 * K, LANE)[...] for k in range(width)]
+        w = [gu[t + k] for k in range(width)]
         w = w[0] if width == 1 else jnp.concatenate(w, axis=1)
         return mm(xp[e], w)
 
@@ -335,9 +343,9 @@
         @pl.loop(0, SIDE // 2)
         def _(p):
             at = pl.ds(pl.multiple_of(p * 2 * LANE, 2 * LANE), 2 * LANE)
-            store(at, product(e, h, p, 2))
-
-        store(pl.ds((SIDE - 1) * LANE, LANE), product(e, h, SIDE // 2, 1))
+            store(p, at, product(e, h, p, 2))
+
+        store(SIDE // 2, pl.ds((SIDE - 1) * LANE, LANE), product(e, h, SIDE // 2, 1))
 
     def arrive(e):
         @pl.loop(0, TILES)
@@ -347,7 +355,7 @@
     arrive(1 - c)
     for n, h in enumerate((1 - x, x)):
 
-        def to_sibling(at, r, n=n):
+        def to_sibling(p, at, r, n=n):
             l1_send[n, :, at] = bf(r)
 
         sweep(1 - c, h, to_sibling)
@@ -360,37 +368,53 @@
     first = remote(l1_send.at[0], l1_recv.at[0], l1_ss.at[0], l1_rs.at[0], sibling)
     first.wait_recv()
 
-    def to_across(at, r):
+    def l2(p, at):
+        return remote(l2_send.at[:, at], l2_recv.at[:, at], l2_ss.at[p], l2_rs.at[p], across)
+
+    def h_acr(p, at, side):
+        ref = hid.at[c, side, :, at]
+        return remote(ref, ref, h_ss.at[p], h_rs.at[p], across)
+
+    def h_fwd(p, at, e):
+        ref = hid.at[e, 1 - x, :, at]
+        return remote(ref, ref, f_ss.at[p], f_rs.at[p], sibling)
+
+    def each(do):
+        @pl.loop(0, SIDE // 2)
+        def _(p):
+            do(p, pl.ds(pl.multiple_of(p * 2 * LANE, 2 * LANE), 2 * LANE), 2 * LANE)
+
+        do(SIDE // 2, pl.ds((SIDE - 1) * LANE, LANE), LANE)
+
+    def to_across(p, at, r):
         l2_send[:, at] = bf(r + f32(l1_recv[0, :, at]))
+        l2(p, at).start()
 
     sweep(c, 1 - x, to_across)
-    l2 = remote(l2_send, l2_recv, l2_ss, l2_rs, across)
-    l2.start()
     second = remote(l1_send.at[1], l1_recv.at[1], l1_ss.at[1], l1_rs.at[1], sibling)
     second.wait_recv()
 
-    def to_own(at, r):
+    def to_own(p, at, r):
         acc[:, at] = r + f32(l1_recv[1, :, at])
 
     sweep(c, x, to_own)
     s_two.wait_recv()
     scale = lax.rsqrt((s_mine[c] + s_recv[1])[0:SLOTS, 0:1] / D + 1e-05)
-    l2.wait_recv()
-
-    @pl.loop(0, SIDE)
-    def _(t):
-        at = pl.ds(pl.multiple_of(t * LANE, LANE), LANE)
+
+    def activate(p, at, width):
+        l2(p, at).wait_recv()
         total = acc[:, at] + f32(l2_recv[:, at])
         gate, up = total[0:SLOTS] * scale, total[SLOTS : 2 * SLOTS] * scale
         value = gate / (1.0 + jnp.exp(-gate)) * up
-        value = jnp.where(jnp.logical_and(t == 0, x == 1), 0.0, value)
+        column = lax.broadcasted_iota(jnp.int32, (SLOTS, width), 1) + p * 2 * LANE
+        value = jnp.where(jnp.logical_and(x == 1, column < LANE), 0.0, value)
         hid[c, x, :, at] = bf(
-            jnp.concatenate([value, jnp.zeros((64 - SLOTS, LANE), jnp.float32)], axis=0)
+            jnp.concatenate([value, jnp.zeros((64 - SLOTS, width), jnp.float32)], axis=0)
         )
-
-    h_sib = remote(hid.at[c, x], hid.at[c, x], h_ss.at[0], h_rs.at[0], sibling)
-    h_acr = remote(hid.at[c, x], hid.at[c, x], h_ss.at[1], h_rs.at[1], across)
-    h_acr.start()
+        h_acr(p, at, x).start()
+
+    each(activate)
+    h_sib = remote(hid.at[c, x], hid.at[c, x], hs_ss, hs_rs, sibling)
     h_sib.start()
     for e in range(EXP_WIN):
         wd_copy(e).wait()
@@ -404,12 +428,15 @@
     h_sib.wait_recv()
     for n in range(3):
         outs[1 - c, :, 512 * n : 512 * (n + 1)] = down(1 - c, x, n)
-    h_acr.wait_recv()
-    h_fwd = remote(hid.at[c, 1 - x], hid.at[c, 1 - x], h_ss.at[2], h_rs.at[2], sibling)
-    h_fwd.start()
+
+    def forward(p, at, width):
+        h_acr(p, at, 1 - x).wait_recv()
+        h_fwd(p, at, c).start()
+
+    each(forward)
     for n in range(3):
         outs[c, :, 512 * n : 512 * (n + 1)] += down(c, 1 - x, n)
-    h_fwd.wait_recv()
+    each(lambda p, at, width: h_fwd(p, at, 1 - c).wait_recv())
     for n in range(3):
         outs[1 - c, :, 512 * n : 512 * (n + 1)] += down(1 - c, 1 - x, n)
 
@@ -448,8 +475,15 @@
     def _():
         remote(a_send, a_recv.at[i], a_ss.at[0], a_rs.at[i], sibling).wait_send()
 
-    for copy in (s_one, s_two, first, second, l2, h_sib, h_acr, h_fwd):
+    for copy in (s_one, s_two, first, second, h_sib):
         copy.wait_send()
+
+    def left(p, at, width):
+        l2(p, at).wait_send()
+        h_acr(p, at, x).wait_send()
+        h_fwd(p, at, c).wait_send()
+
+    each(left)
 
 
 def attention(queries, cached_key_rows, cached_value_rows, lengths):
@@ -509,7 +543,7 @@
     dma = pltpu.SemaphoreType.DMA
     scratch = [
         pltpu.VMEM((K, K), b16),
-        pltpu.VMEM((EXP_WIN * TILES, K, 2, LANE), b16),
+        pltpu.VMEM((EXP_WIN * TILES, 2 * K, LANE), b16),
         pltpu.VMEM((EXP_WIN, TILES * LANE, K), b16),
         pltpu.VMEM((PAIR, HALF), b16),
         pltpu.VMEM((N, PAIR, HALF), b16),
@@ -536,7 +570,8 @@
         dma((EXP_WIN * TILES,)),
         dma((EXP_WIN,)),
     ]
-    scratch += [dma((N,))] * 10 + [dma((2,))] * 4 + [dma, dma] + [dma((3,))] * 2 + [dma((N,))] * 2
+    scratch += [dma((N,))] * 10 + [dma((2,))] * 4 + [dma((6,))] * 2
+    scratch += [dma, dma] + [dma((6,))] * 4 + [dma((N,))] * 2
     return pl.pallas_call(
         fused,
         out_shape=jax.ShapeDtypeStruct((ROWS, K), b16),

time: 90.3 us -> 79.1 us (0.88)
  Pallas kernels: 81 us -> 69.8 us
    pallas_call x1, Pallas kernels: 81 us -> 69.8 us  [fused_local(): pl.pallas_call(fused, out_shape=jax.ShapeDtypeStruct((ROWS, K), b16), in_...]
where the time goes in v2:
time: 79.1 us; the launch traced here: 78.8 us
  Pallas kernels  69.8 us (88%)
  local copies, waits for them, and re-layouts  4.15 us (5%)
  matrix products  3 us (4%)
  other arithmetic  1.85 us (2%)
    pallas_call x1, Pallas kernels, fused_local(): pl.pallas_call(fused, out_shape=jax.ShapeDtypeStruct((ROWS, K), b16), in_...  69.8 us
    dot_general x1, matrix products, attention(): jnp.einsum('tkgd,tskd->tkgs', per_head_queries, per_head_keys, preferred_...  2.31 us

profile of v2, /device:TPU:0, one launch (start us, length us, event | category | flops | bytes accessed | tf_op | source)
XLA Modules:
  0.0 78.8 jit_solution(10921420701739085422)
XLA Ops:
  0.0 0.0 copy-start.3
  0.0 1.1 %reshape.62 = bf16[24,2,6,128]{3,2,1,0:T(8,128)(2,1)S(1)} reshape(bf16[24,1536]{1,0:T(8,128)(2,1)} %param.11) | data formatting | bytes 147456 | tf_op jit(solution)/shard_map/reshape | solution.py:495
  1.1 0.7 iota_compare_fusion.2
  1.8 2.3 %fusion.11 = f32[24,2,6,128]{3,2,1,0:T(8,128)S(1)} fusion(bf16[24,2,6,128]{3,2,1,0:T(8,128)(2,1)S(1)} %reshape.62, pred[24,128]{1,0:T(8,128)(4,1)S(1)} %iota_compare_fusion.2, bf16[24,128,256]{2,1,0:T(8,128)(2,1)} %param.12), kind=kOutput, calls=%fused_computation.9 | convolution fusion | flops 9510912 | bytes 1797120 | tf_op jit(solution)/shard_map/tkgd,tskd->tkgs/dot_general | solution.py:498
  4.2 0.0 copy-start.1
  4.2 0.0 copy-start.2
  4.2 0.0 copy-start
  4.2 0.3 fusion.20
  4.4 0.0 copy-done.3
  4.4 0.7 fusion.15
  5.1 0.7 reshape.65.att_ref
  5.9 0.0 copy-done.1
  5.9 0.1 convert_reduce_fusion
  6.0 0.1 eq.34
  6.1 0.1 compare_convert_fusion
  6.2 0.0 copy-done.2
  6.2 0.1 copy.24
  6.3 0.6 select_maximum_fusion.meta_ref
  6.9 0.0 copy-done
  6.9 0.6 broadcast_in_dim.26.gain_ref
  7.5 69.8 %shard_map.109 = bf16[24,1536]{1,0:T(8,128)(2,1)} custom-call(bf16[24,1536]{1,0:T(8,128)(2,1)} %reshape.65.att_ref, f32[72,128]{1,0:T(8,128)} %select_maximum_fusion.meta_ref, bf16[24,1536]{1,0:T(8,128)(2,1)} %res_ref.1, f32[1,1536]{1,0:T(1,128)} %broadcast_in_dim.26.gain_ref, bf16[1536,1536]{1,0:T(8,128)(2,1)} %wo_hbm.1, bf16[2,1536,2,2688]{3,2,1,0:T(2,128)(2,1)} %gu_hbm.1, ...), custom_call_target="tpu_custom_call" | custom-call | tf_op jit(solution)/shard_map/pallas_call | solution.py:575
  77.3 1.5 %copy.42 = bf16[24,1536]{1,0:T(8,128)(2,1)} copy(bf16[24,1536]{1,0:T(8,128)(2,1)} %shard_map.109) | data formatting | bytes 147456
  (5 shorter events, 0.1 us)
Async XLA Ops:
  0.0 4.4 %copy-start.3 = (bf16[24,128,256]{2,1,0:T(8,128)(2,1)S(1)}, bf16[24,128,256]{2,1,0:T(8,128)(2,1)}, u32[]{:S(2)}) copy-start(bf16[24,128,256]{2,1,0:T(8,128)(2,1)} %param.13) | copy-start | bytes 4718596
  4.2 1.7 %copy-start.1 = (s32[24,4]{0,1:T(4,128)S(1)}, s32[24,4]{0,1:T(4,128)}, u32[]{:S(2)}) copy-start(s32[24,4]{0,1:T(4,128)} %param.18) | copy-start | bytes 1156
  4.2 2.0 %copy-start.2 = (f32[24,4]{0,1:T(4,128)S(1)}, f32[24,4]{0,1:T(4,128)}, u32[]{:S(2)}) copy-start(f32[24,4]{0,1:T(4,128)} %param.19) | copy-start | bytes 1156
  4.2 2.8 %copy-start = (f32[1536]{0:T(1024)S(1)}, f32[1536]{0:T(1024)}, u32[]{:S(2)}) copy-start(f32[1536]{0:T(1024)} %param.17) | copy-start | bytes 18436

commit v3 on v2

--- a/solution.py
+++ b/solution.py
@@ -276,13 +276,36 @@
     stream[...] = f32(res_ref[...]) + part[mine, :]
     for d in (1, 3, 2):
         s = (i + d) % N
+        remote(meta_all.at[s], meta_all.at[s], m_ss.at[d], m_rs.at[s], sibling).wait_recv()
+    gain = jnp.concatenate([gain_ref[q : q + 1, :] for q in range(K // LANE)], axis=1)
+    twice = bf(
+        lax.broadcasted_iota(jnp.int32, (LANE, 2 * LANE), 1) // 2
+        == lax.broadcasted_iota(jnp.int32, (LANE, 2 * LANE), 0)
+    )
+    keep = (
+        lax.broadcasted_iota(jnp.int32, (2 * SLOTS, 2 * LANE), 1) % 2
+        == lax.broadcasted_iota(jnp.int32, (2 * SLOTS, 2 * LANE), 0) // SLOTS
+    )
+
+    def spots(e):
+        return jnp.concatenate(
+            [meta_all[k, ROWS * e : ROWS * (e + 1), :] for k in range(N)], axis=0
+        )
+
+    fill = jnp.zeros((LANE - N * ROWS, LANE), jnp.float32)
+    places = [
+        jnp.transpose(jnp.concatenate([spots(e), fill], axis=0))[0 : 2 * SLOTS, 0 : N * ROWS]
+        for e in range(EXP_WIN)
+    ]
+    for d in (1, 3, 2):
+        s = (i + d) % N
         remote(rs_send.at[s], rs_recv.at[s], rs_ss.at[d], rs_rs.at[s], sibling).wait_recv()
         got = f32(rs_recv[s])
         stream[:, 0:HALF] += got[0:ROWS]
         stream[:, HALF:K] += got[ROWS:PAIR]
 
     st = stream[...]
-    y = bf(st * gain_ref[...])
+    y = bf(st * gain)
     y_all[i] = jnp.concatenate([y[:, 0:HALF], y[:, HALF:K]], axis=0)
     ss_all[i] = jnp.broadcast_to(jnp.sum(st * st, axis=1, keepdims=True), (ROWS, LANE))
     for d in (2, 1, 3):
@@ -291,7 +314,6 @@
         remote(ss_all.at[i], ss_all.at[i], q_ss.at[d], q_rs.at[i], dev).start()
     for d in (1, 3, 2):
         s = (i + d) % N
-        remote(meta_all.at[s], meta_all.at[s], m_ss.at[d], m_rs.at[s], sibling).wait_recv()
         remote(ss_all.at[s], ss_all.at[s], q_ss.at[d], q_rs.at[s], sibling).wait_recv()
         remote(y_all.at[s], y_all.at[s], y_ss.at[d], y_rs.at[s], sibling).wait_recv()
 
@@ -300,25 +322,8 @@
         for h in range(2)
     ]
     ssd = jnp.concatenate([ss_all[k] for k in range(N)], axis=0)
-    twice = bf(
-        lax.broadcasted_iota(jnp.int32, (LANE, 2 * LANE), 1) // 2
-        == lax.broadcasted_iota(jnp.int32, (LANE, 2 * LANE), 0)
-    )
-    keep = (
-        lax.broadcasted_iota(jnp.int32, (2 * SLOTS, 2 * LANE), 1) % 2
-        == lax.broadcasted_iota(jnp.int32, (2 * SLOTS, 2 * LANE), 0) // SLOTS
-    )
-
-    def spots(e):
-        return jnp.concatenate(
-            [meta_all[k, ROWS * e : ROWS * (e + 1), :] for k in range(N)], axis=0
-        )
-
     for e in range(EXP_WIN):
-        place = spots(e)
-        place_t = jnp.transpose(
-            jnp.concatenate([place, jnp.zeros((LANE - N * ROWS, LANE), jnp.float32)], axis=0)
-        )[0 : 2 * SLOTS, 0 : N * ROWS]
+        place_t = places[e]
         s_mine[e] = jnp.dot(
             place_t, ssd, precision=lax.Precision.HIGHEST, preferred_element_type=jnp.float32
         )
@@ -460,7 +465,7 @@
         got = f32(c_recv[s])
         stream[:, 0:HALF] += got[0:ROWS]
         stream[:, HALF:K] += got[ROWS:PAIR]
-    out_ref[...] = bf(stream[...])
+    out_ref[...] = stream[...]
 
     for d in (1, 2, 3):
         remote(a_send, a_recv.at[i], a_ss.at[d], a_rs.at[i], sibling).wait_send()
@@ -574,14 +579,14 @@
     scratch += [dma, dma] + [dma((6,))] * 4 + [dma((N,))] * 2
     return pl.pallas_call(
         fused,
-        out_shape=jax.ShapeDtypeStruct((ROWS, K), b16),
+        out_shape=jax.ShapeDtypeStruct((ROWS, K), f4),
         in_specs=[vmem] * 4 + [hbm] * 3,
         out_specs=vmem,
         scratch_shapes=scratch,
         compiler_params=pltpu.CompilerParams(
             collective_id=0, has_side_effects=True, vmem_limit_bytes=VMEM_BYTES
         ),
-    )(attended, meta, residual, norm_gain[None, :], out_weight, gate_up_weight, down_weight)
+    )(attended, meta, residual, norm_gain.reshape(K // LANE, LANE), out_weight, gate_up_weight, down_weight).astype(b16)
 
 
 VMEM_BYTES = 63 << 20

time: 79.1 us -> 78.5 us (level)
  local copies, waits for them, and re-layouts: 4.15 us -> 2.03 us
  other arithmetic: 1.85 us -> 3.4 us
    convert_element_type x0 -> x1, other arithmetic: none -> 1.55 us  [fused_local(): return pl.pallas_call(fused, out_shape=jax.ShapeDtypeStruct((ROWS, K), f4...]
    unnamed x9 -> x6, local copies, waits for them, and re-layouts: 1.54 us -> 0.01 us
where the time goes in v3:
time: 78.5 us; the launch traced here: 78.2 us
  Pallas kernels  69.8 us (89%)
  other arithmetic  3.4 us (4%)
  matrix products  3 us (4%)
  local copies, waits for them, and re-layouts  2.03 us (3%)
    pallas_call x1, Pallas kernels, fused_local(): pl.pallas_call(fused, out_shape=jax.ShapeDtypeStruct((ROWS, K), f4), in_s...  69.8 us
    dot_general x1, matrix products, attention(): jnp.einsum('tkgd,tskd->tkgs', per_head_queries, per_head_keys, preferred_...  2.31 us

profile of v3, /device:TPU:0, one launch (start us, length us, event | category | flops | bytes accessed | tf_op | source)
XLA Modules:
  0.0 78.2 jit_solution(936478063991962167)
XLA Ops:
  0.0 0.0 copy-start.2
  0.0 1.1 %reshape.65 = bf16[24,2,6,128]{3,2,1,0:T(8,128)(2,1)S(1)} reshape(bf16[24,1536]{1,0:T(8,128)(2,1)} %param.11) | data formatting | bytes 147456 | tf_op jit(solution)/shard_map/reshape | solution.py:500
  1.1 0.7 iota_compare_fusion.2
  1.8 2.3 %fusion.11 = f32[24,2,6,128]{3,2,1,0:T(8,128)S(1)} fusion(bf16[24,2,6,128]{3,2,1,0:T(8,128)(2,1)S(1)} %reshape.65, pred[24,128]{1,0:T(8,128)(4,1)S(1)} %iota_compare_fusion.2, bf16[24,128,256]{2,1,0:T(8,128)(2,1)} %param.12), kind=kOutput, calls=%fused_computation.9 | convolution fusion | flops 9510912 | bytes 1797120 | tf_op jit(solution)/shard_map/tkgd,tskd->tkgs/dot_general | solution.py:503
  4.2 0.0 copy-start
  4.2 0.0 copy-start.1
  4.2 0.3 fusion.20
  4.4 0.0 copy-done.2
  4.4 0.7 fusion.15
  5.1 0.7 reshape.68.att_ref
  5.9 0.0 copy-done
  5.9 0.1 convert_reduce_fusion
  6.0 0.1 eq.34
  6.1 0.1 compare_convert_fusion
  6.2 0.0 copy-done.1
  6.2 0.1 copy.24
  6.3 0.6 select_maximum_fusion.meta_ref
  6.9 69.8 %shard_map.109 = f32[24,1536]{1,0:T(8,128)} custom-call(bf16[24,1536]{1,0:T(8,128)(2,1)} %reshape.68.att_ref, f32[72,128]{1,0:T(8,128)} %select_maximum_fusion.meta_ref, bf16[24,1536]{1,0:T(8,128)(2,1)} %res_ref.1, f32[12,128]{1,0:T(8,128)} %bitcast.26, bf16[1536,1536]{1,0:T(8,128)(2,1)} %wo_hbm.1, bf16[2,1536,2,2688]{3,2,1,0:T(2,128)(2,1)} %gu_hbm.1, ...), custom_call_target="tpu_custom_call" | custom-call | tf_op jit(solution)/shard_map/pallas_call | solution.py:580
  76.7 1.6 %convert_element_type.23 = bf16[24,1536]{1,0:T(8,128)(2,1)} convert(f32[24,1536]{1,0:T(8,128)} %shard_map.109) | non-fusion elementwise | flops 36864 | bytes 221184 | tf_op jit(solution)/shard_map/convert_element_type | solution.py:589
  (5 shorter events, 0.1 us)
Async XLA Ops:
  0.0 4.4 %copy-start.2 = (bf16[24,128,256]{2,1,0:T(8,128)(2,1)S(1)}, bf16[24,128,256]{2,1,0:T(8,128)(2,1)}, u32[]{:S(2)}) copy-start(bf16[24,128,256]{2,1,0:T(8,128)(2,1)} %param.13) | copy-start | bytes 4718596
  4.2 1.7 %copy-start = (s32[24,4]{0,1:T(4,128)S(1)}, s32[24,4]{0,1:T(4,128)}, u32[]{:S(2)}) copy-start(s32[24,4]{0,1:T(4,128)} %param.18) | copy-start | bytes 1156
  4.2 2.0 %copy-start.1 = (f32[24,4]{0,1:T(4,128)S(1)}, f32[24,4]{0,1:T(4,128)}, u32[]{:S(2)}) copy-start(f32[24,4]{0,1:T(4,128)} %param.19) | copy-start | bytes 1156
